TPU v7x, 32 devices: a whole 2x2x4 slice. The times are simulated.
32 devices in a mesh: seq: 8 (over y, x, core), head: 4 (over z).
Axes of the slice: x: 2, y: 2, z: 4, core: 2. Of those that a mesh axis runs over, the one named last changes fastest.
Arguments:
- queries: bfloat16 [16384, 2048], P('seq', 'head'), may hold values from -4.5 to 4.5
- key_vectors: bfloat16 [16384, 2048], P('seq', 'head'), may hold values from -4.5 to 4.5
- value_vectors: bfloat16 [16384, 2048], P('seq', 'head'), may hold values from -18 to 18
- w_out: bfloat16 [2048, 2048], P('seq'), may hold values from -0.125 to 0.125
Outputs:
- projected: bfloat16 [16384, 2048], P(('seq', 'head'))
All inputs are finite; a program needn't handle non-finite values.
Results may differ from a plain program's by a relative error of at most 0.0053.
Values may be sent and summed in bfloat16 or wider, within the bound.
A program may use at most 128 MiB of HBM per device.

v0:
```python
import math

import jax
import jax.numpy as jnp
from jax import lax
from jax.sharding import PartitionSpec as P

HD = 128
W = 1024


norm_eps = 1e-06


def passed_along(shard, axis, by):
    count = lax.axis_size(axis)
    pairs = [(i, i + by) for i in range(count) if 0 <= i + by < count]
    return lax.ppermute(shard, axis, pairs)


def carried_in(part, axis, combine, identity):
    place = lax.axis_index(axis)
    gathered = lax.all_gather(part, axis)
    state = jnp.zeros_like(part) + jnp.asarray(identity, part.dtype)

    def one(lap, state):
        return combine(state, lax.dynamic_index_in_dim(gathered, lap, 0, False))

    return lax.fori_loop(0, place, one, state)


def normalize(branch):
    return branch * lax.rsqrt(jnp.mean(branch * branch, axis=-1, keepdims=True) + norm_eps)


def add_states(earlier, later):
    return earlier + later


def split_pair(values):
    upper = lax.optimization_barrier(values.astype(jnp.bfloat16))
    lower = (values - upper.astype(jnp.float32)).astype(jnp.bfloat16)
    return (upper, lower)


def window_branch(query_heads, window_keys, window_values, offset):
    tok_rows, heads_here, head_width = query_heads.shape
    block_rows = min(512, tok_rows)
    key_span = block_rows + W
    score_scale = 1.0 / math.sqrt(head_width)

    def one_block(block_start):
        query_block = lax.dynamic_slice_in_dim(query_heads, block_start, block_rows, 0)
        key_block = lax.dynamic_slice_in_dim(window_keys, block_start, key_span, 0)
        value_block = lax.dynamic_slice_in_dim(window_values, block_start, key_span, 0)
        scores = (
            jnp.einsum("qhd,khd->hqk", query_block, key_block, preferred_element_type=jnp.float32)
            * score_scale
        )
        row_index = block_start + jnp.arange(block_rows, dtype=jnp.int32)[:, None]
        col_index = block_start + jnp.arange(key_span, dtype=jnp.int32)[None, :]
        allowed = (
            (col_index > row_index) & (col_index <= row_index + W) & (col_index - W + offset >= 0)
        )
        scores = jnp.where(allowed[None], scores, -jnp.inf)
        row_top = jnp.max(scores, axis=-1, keepdims=True)
        weights = jnp.where(allowed[None], jnp.exp(scores - row_top), 0.0).astype(jnp.bfloat16)
        return jnp.einsum("hqk,khd->qhd", weights, value_block, preferred_element_type=jnp.float32)

    starts = jnp.arange(tok_rows // block_rows, dtype=jnp.int32) * block_rows
    return lax.map(one_block, starts).reshape(tok_rows, heads_here, head_width)


def on_device(queries, key_vectors, value_vectors, w_out):
    tok_rows = queries.shape[0]
    heads_here = queries.shape[1] // HD
    head_shape = (tok_rows, heads_here, HD)
    query_heads = queries.reshape(head_shape)
    key_heads = key_vectors.reshape(head_shape)
    value_heads = value_vectors.reshape(head_shape)
    window_rim = jnp.stack([key_heads[tok_rows - W :], value_heads[tok_rows - W :]])
    earlier = passed_along(window_rim, "seq", 1)
    window_keys = jnp.concatenate([earlier[0], key_heads], axis=0)
    window_values = jnp.concatenate([earlier[1], value_heads], axis=0)
    offset = lax.axis_index("seq") * tok_rows
    soft_heads = window_branch(query_heads, window_keys, window_values, offset)
    block_rows = min(512, tok_rows)
    block_count = tok_rows // block_rows
    block_shape = (block_count, block_rows, heads_here, HD)
    blocked_queries = query_heads.reshape(block_shape)
    blocked_keys = key_heads.reshape(block_shape)
    blocked_values = value_heads.reshape(block_shape)
    state_increments = jnp.einsum(
        "bkhd,bkhe->bhde", blocked_keys, blocked_values, preferred_element_type=jnp.float32
    )
    own_total = jnp.sum(state_increments, axis=0)
    prior_state = carried_in(own_total, "seq", add_states, jnp.zeros_like(own_total))
    running = jnp.cumsum(state_increments, axis=0)
    preceding_state = prior_state[None] + jnp.concatenate(
        [jnp.zeros_like(state_increments[:1]), running[:-1]], axis=0
    )
    intra_block_scores = jnp.einsum(
        "bqhd,bkhd->bhqk", blocked_queries, blocked_keys, preferred_element_type=jnp.float32
    )
    causal = (
        jnp.arange(block_rows, dtype=jnp.int32)[:, None]
        >= jnp.arange(block_rows, dtype=jnp.int32)[None, :]
    )
    intra_block_scores = jnp.where(causal, intra_block_scores, 0.0)
    score_upper, score_lower = split_pair(intra_block_scores)
    local_block_terms = jnp.einsum(
        "bhqk,bkhd->bqhd", score_upper, blocked_values, preferred_element_type=jnp.float32
    )
    local_block_terms = local_block_terms + jnp.einsum(
        "bhqk,bkhd->bqhd", score_lower, blocked_values, preferred_element_type=jnp.float32
    )
    state_upper, state_lower = split_pair(preceding_state)
    carried_state_sum = jnp.einsum(
        "bqhd,bhde->bqhe", blocked_queries, state_upper, preferred_element_type=jnp.float32
    )
    carried_state_sum = carried_state_sum + jnp.einsum(
        "bqhd,bhde->bqhe", blocked_queries, state_lower, preferred_element_type=jnp.float32
    )
    linear = (local_block_terms + carried_state_sum).reshape(head_shape)
    mixed_heads = (0.5 * (normalize(soft_heads) + normalize(linear))).astype(jnp.bfloat16)
    mixed_heads = mixed_heads.reshape(tok_rows, heads_here * HD)
    regrouped = lax.all_to_all(mixed_heads, "head", split_axis=0, concat_axis=1, tiled=True)
    projected = jnp.dot(
        regrouped,
        lax.all_gather(w_out, "seq", axis=0, tiled=True),
        preferred_element_type=jnp.float32,
    )
    return projected.astype(jnp.bfloat16)


def solution(mesh):
    placed = (P("seq", "head"), P("seq", "head"), P("seq", "head"), P("seq", None))
    return jax.shard_map(
        on_device, mesh=mesh, in_specs=placed, out_specs=P(("seq", "head"), None), check_vma=False
    )
```

profile of v0, /device:TPU:0, one launch (start us, length us, event | category | flops | bytes accessed | tf_op | source)
XLA Modules:
  0.0 312.2 jit_solution(3316408791350834074)
XLA Ops:
  6.5 2.5 reshape_reshape.10
  9.1 2.6 copy.89
  11.7 2.5 reshape_reshape.11
  14.2 4.8 %fusion.44 = (f32[4,128,128]{2,1,0:T(8,128)}, f32[4,4,128,128]{3,2,1,0:T(8,128)}) fusion(bf16[4,512,4,128]{1,3,2,0:T(8,128)(2,1)} %copy.89, bf16[4,512,4,128]{3,2,1,0:T(4,128)(2,1)S(1)} %reshape_reshape.11), kind=kOutput, calls=%fused_computation.61 | convolution fusion | flops 268632064 | bytes 5505024 | tf_op jit(solution)/shard_map/bkhd,bkhe->bhde/dot_general | solution.py:93
  19.1 4.0 %copy.76 = bf16[2048,512]{0,1:T(8,128)(2,1)} copy(bf16[2048,512]{1,0:T(8,128)(2,1)} %param.9) | data formatting | bytes 4194304 | tf_op args[1]
  23.0 4.1 %copy.77 = bf16[2048,512]{0,1:T(8,128)(2,1)} copy(bf16[2048,512]{1,0:T(8,128)(2,1)} %param.10) | data formatting | bytes 4194304 | tf_op args[2]
  27.1 1.2 slice-done.1
  28.4 1.6 pad_maximum_fusion.2
  29.9 3.7 %collective-permute-start = (bf16[2,1024,4,128]{1,3,2,0:T(8,128)(2,1)}, bf16[2,1024,4,128]{1,3,2,0:T(8,128)(2,1)}, u32[]{:S(2)}, u32[]{:S(2)}) collective-permute-start(bf16[2,1024,4,128]{1,3,2,0:T(8,128)(2,1)} %pad_maximum_fusion.2), channel_id=1, source_target_pairs={{0,4},{4,8},{8,12},{12,16},{16,20},{20,24},{24,28},{1,5},{5,9},{9,... | collective-permute-start | bytes 6291464 | tf_op jit(solution)/shard_map/ppermute | solution.py:18
  33.7 2.6 reshape_reshape.9
  36.3 4.0 %copy.79 = bf16[2048,512]{0,1:T(8,128)(2,1)} copy(bf16[2048,512]{1,0:T(8,128)(2,1)} %param.8) | data formatting | bytes 4194304 | tf_op args[0]
  40.3 11.3 %select_convert_fusion.1 = (bf16[4,4,512,512]{3,2,1,0:T(8,128)(2,1)}, f32[4,4,512,512]{3,2,1,0:T(8,128)}) fusion(pred[512,512]{1,0:T(8,128)(4,1)S(1)} %iota_compare_fusion, bf16[4,512,4,128]{1,3,2,0:T(8,128)(2,1)} %copy.89, bf16[4,512,4,128]{3,2,1,0:T(4,128)(2,1)S(1)} %reshape_reshape.9), kind=kOutput, calls=%fused_computation.27 | convolution fusion | flops 1077936128 | bytes 29622272 | tf_op jit(solution)/shard_map/bqhd,bkhd->bhqk/dot_general | solution.py:102
  51.5 12.9 %fusion.27 = f32[4,4,512,128]{2,3,1,0:T(8,128)} fusion(bf16[4,4,512,512]{3,2,1,0:T(8,128)(2,1)} %get-tuple-element.175, f32[4,4,512,512]{3,2,1,0:T(8,128)} %get-tuple-element.176, pred[512,512]{1,0:T(8,128)(4,1)S(1)} %iota_compare_fusion, bf16[4,512,4,128]{3,2,1,0:T(4,128)(2,1)} %copy-done), kind=kOutput, calls=%fused_computation.28 | convolution fusion | flops 1090519040 | bytes 31719424 | tf_op jit(solution)/shard_map/bhqk,bkhd->bqhd/dot_general | solution.py:114
  64.4 0.7 fusion.45
  65.1 0.9 slice.26
  66.0 8.8 %fusion.31 = f32[4,4,512,128]{2,3,1,0:T(8,128)} fusion(bf16[4,4,512,512]{3,2,1,0:T(8,128)(2,1)} %get-tuple-element.175, bf16[4,512,4,128]{3,2,1,0:T(4,128)(2,1)} %copy-done), kind=kOutput, calls=%fused_computation.40 | convolution fusion | flops 1073741824 | bytes 14680064 | tf_op jit(solution)/shard_map/bhqk,bkhd->bqhd/dot_general | solution.py:111
  74.8 1.9 slice_bitcast_fusion
  77.7 2.9 pad_maximum_fusion
  80.5 108.9 %while.22 = (s32[]{:T(128)}, f32[4,512,4,128]{1,3,2,0:T(8,128)}, s32[4]{0:T(128)S(1)}, bf16[3072,4,128]{0,2,1:T(8,128)(2,1)}, s32[]{:T(128)}, /*index=5*/bf16[20...) while((s32[]{:T(128)}, f32[4,512,4,128]{1,3,2,0:T(8,128)}, ...), condition=%wide.region_2.3_spmd, body=%wide.region_0.2_spmd.sunk | while | flops 1635790848 | bytes 44850896 | solution.py:71
  84.3 8.2 %fusion.61 = f32[4,512,1536]{2,1,0:T(8,128)} fusion(bf16[3072,4,128]{0,2,1:T(8,128)(2,1)} %get-tuple-element.303, s32[]{:T(128)S(6)} %select_n.74, bf16[2048,4,128]{0,2,1:T(8,128)(2,1)} %get-tuple-element.302, s32[]{:T(128)S(6)} %select_n.75), kind=kOutput, calls=%fused_computation.10.clone.1 | convolution fusion | flops 805306368 | bytes 14680072 | tf_op jit(solution)/shard_map/while/body/eval_jaxpr/qhd,khd->hqk/dot_general | solution.py:57
  94.4 0.8 and_and_fusion.2
  95.2 12.8 %fusion.62 = f32[4,512,4,128]{1,3,2,0:T(8,128)} fusion(f32[4,512,4,128]{1,3,2,0:T(8,128)} %get-tuple-element.287, s32[]{:T(128)} %get-tuple-element.286, f32[4,512,1536]{2,1,0:T(8,128)} %fusion.61, pred[512,1536]{1,0:T(8,128)(4,1)S(1)} %and_and_fusion.2, bf16[3072,4,128]{0,2,1:T(8,128)(2,1)} %get-tuple-element.300, s32[]{:T(128)S(6)} %select_n.74), kind=kOutput, calls=%fused_computation.14.clone.1 | convolution fusion | flops 827330048 | bytes 29360644 | tf_op jit(solution)/shard_map/while/body/eval_jaxpr/hqk,khd->qhd/dot_general | solution.py:68
  111.8 8.2 %fusion.61 = f32[4,512,1536]{2,1,0:T(8,128)} fusion(bf16[3072,4,128]{0,2,1:T(8,128)(2,1)} %get-tuple-element.303, s32[]{:T(128)S(6)} %select_n.74, bf16[2048,4,128]{0,2,1:T(8,128)(2,1)} %get-tuple-element.302, s32[]{:T(128)S(6)} %select_n.75), kind=kOutput, calls=%fused_computation.10.clone.1 | convolution fusion | flops 805306368 | bytes 14680072 | tf_op jit(solution)/shard_map/while/body/eval_jaxpr/qhd,khd->hqk/dot_general | solution.py:57
  120.6 0.6 add_compare_fusion.2
  121.9 0.8 and_and_fusion.2
  122.6 12.5 %fusion.62 = f32[4,512,4,128]{1,3,2,0:T(8,128)} fusion(f32[4,512,4,128]{1,3,2,0:T(8,128)} %get-tuple-element.287, s32[]{:T(128)} %get-tuple-element.286, f32[4,512,1536]{2,1,0:T(8,128)} %fusion.61, pred[512,1536]{1,0:T(8,128)(4,1)S(1)} %and_and_fusion.2, bf16[3072,4,128]{0,2,1:T(8,128)(2,1)} %get-tuple-element.300, s32[]{:T(128)S(6)} %select_n.74), kind=kOutput, calls=%fused_computation.14.clone.1 | convolution fusion | flops 827330048 | bytes 29360644 | tf_op jit(solution)/shard_map/while/body/eval_jaxpr/hqk,khd->qhd/dot_general | solution.py:68
  139.0 8.2 %fusion.61 = f32[4,512,1536]{2,1,0:T(8,128)} fusion(bf16[3072,4,128]{0,2,1:T(8,128)(2,1)} %get-tuple-element.303, s32[]{:T(128)S(6)} %select_n.74, bf16[2048,4,128]{0,2,1:T(8,128)(2,1)} %get-tuple-element.302, s32[]{:T(128)S(6)} %select_n.75), kind=kOutput, calls=%fused_computation.10.clone.1 | convolution fusion | flops 805306368 | bytes 14680072 | tf_op jit(solution)/shard_map/while/body/eval_jaxpr/qhd,khd->hqk/dot_general | solution.py:57
  149.1 0.8 and_and_fusion.2
  149.9 12.6 %fusion.62 = f32[4,512,4,128]{1,3,2,0:T(8,128)} fusion(f32[4,512,4,128]{1,3,2,0:T(8,128)} %get-tuple-element.287, s32[]{:T(128)} %get-tuple-element.286, f32[4,512,1536]{2,1,0:T(8,128)} %fusion.61, pred[512,1536]{1,0:T(8,128)(4,1)S(1)} %and_and_fusion.2, bf16[3072,4,128]{0,2,1:T(8,128)(2,1)} %get-tuple-element.300, s32[]{:T(128)S(6)} %select_n.74), kind=kOutput, calls=%fused_computation.14.clone.1 | convolution fusion | flops 827330048 | bytes 29360644 | tf_op jit(solution)/shard_map/while/body/eval_jaxpr/hqk,khd->qhd/dot_general | solution.py:68
  166.3 8.1 %fusion.61 = f32[4,512,1536]{2,1,0:T(8,128)} fusion(bf16[3072,4,128]{0,2,1:T(8,128)(2,1)} %get-tuple-element.303, s32[]{:T(128)S(6)} %select_n.74, bf16[2048,4,128]{0,2,1:T(8,128)(2,1)} %get-tuple-element.302, s32[]{:T(128)S(6)} %select_n.75), kind=kOutput, calls=%fused_computation.10.clone.1 | convolution fusion | flops 805306368 | bytes 14680072 | tf_op jit(solution)/shard_map/while/body/eval_jaxpr/qhd,khd->hqk/dot_general | solution.py:57
  176.3 0.8 and_and_fusion.2
  177.0 12.4 %fusion.62 = f32[4,512,4,128]{1,3,2,0:T(8,128)} fusion(f32[4,512,4,128]{1,3,2,0:T(8,128)} %get-tuple-element.287, s32[]{:T(128)} %get-tuple-element.286, f32[4,512,1536]{2,1,0:T(8,128)} %fusion.61, pred[512,1536]{1,0:T(8,128)(4,1)S(1)} %and_and_fusion.2, bf16[3072,4,128]{0,2,1:T(8,128)(2,1)} %get-tuple-element.300, s32[]{:T(128)S(6)} %select_n.74), kind=kOutput, calls=%fused_computation.14.clone.1 | convolution fusion | flops 827330048 | bytes 29360644 | tf_op jit(solution)/shard_map/while/body/eval_jaxpr/hqk,khd->qhd/dot_general | solution.py:68
  189.5 2.8 multiply_reduce_fusion.1
  192.6 3.9 %mul.55 = f32[2048,4,128]{2,1,0:T(4,128)} broadcast(f32[2048,4]{1,0:T(8,128)S(1)} %copy.84), dimensions={0,1} | broadcast | bytes 4227072 | tf_op jit(solution)/shard_map/mul | solution.py:33
  196.5 5.5 %mul.56 = f32[4,512,512]{2,1,0:T(8,128)} reshape(f32[2048,4,128]{2,1,0:T(4,128)} %mul.55) | data formatting | bytes 8388608 | tf_op jit(solution)/shard_map/mul | solution.py:33
  202.0 5.3 %copy.100 = f32[4,512,512]{2,1,0:T(8,128)} copy(f32[4,512,512]{1,2,0:T(8,128)} %bitcast.43) | data formatting | bytes 8388608 | tf_op jit(solution)/shard_map/reshape | solution.py:71
  207.3 1.1 copy-done.5
  208.5 0.8 fusion.36
  209.3 1.3 copy-done.1
  210.6 1.3 copy-done.2
  211.8 3.6 %multiply_reduce_fusion = (f32[4,512,4]{1,2,0:T(4,128)S(1)}, f32[4,512,4,128]{1,3,2,0:T(8,128)}) fusion(f32[4,4,128,512]{3,2,1,0:T(8,128)S(1)} %fusion.36, bf16[4,512,4,128]{3,2,1,0:T(4,128)(2,1)S(1)} %reshape_reshape.9, bf16[4,4,128,128]{3,2,1,0:T(8,128)(2,1)S(1)} %fusion.40, f32[3,4,128,128]{3,2,1,0:T(8,128)S(1)} %copy-done.5, ...), kind=kOutput, calls=%fused_computation.33 | convolution fusion | flops 274718720 | bytes 20480000 | tf_op jit(solution)/shard_map/bqhd,bhde->bqhe/dot_general | solution.py:121
  215.8 3.9 %mul.59 = f32[2048,4,128]{2,1,0:T(4,128)} broadcast(f32[2048,4]{1,0:T(8,128)S(1)} %copy.95), dimensions={0,1} | broadcast | bytes 4227072 | tf_op jit(solution)/shard_map/mul | solution.py:33
  219.7 5.5 %mul.60 = f32[4,512,512]{2,1,0:T(8,128)} reshape(f32[2048,4,128]{2,1,0:T(4,128)} %mul.59) | data formatting | bytes 8388608 | tf_op jit(solution)/shard_map/mul | solution.py:33
  225.2 5.3 %copy.96 = f32[4,512,512]{2,1,0:T(8,128)} copy(f32[4,512,512]{1,2,0:T(8,128)} %bitcast.42) | data formatting | bytes 8388608 | tf_op jit(solution)/shard_map/reshape | solution.py:124
  230.4 8.0 %multiply_convert_fusion = bf16[4,512,512]{2,1,0:T(8,128)(2,1)S(1)} fusion(f32[4,512,512]{2,1,0:T(8,128)} %copy.96, f32[4,512,512]{2,1,0:T(8,128)} %mul.60, f32[4,512,512]{2,1,0:T(8,128)} %copy.100, f32[4,512,512]{2,1,0:T(8,128)} %mul.56), kind=kLoop, calls=%fused_computation.32 | loop fusion | flops 5242880 | bytes 18874368 | tf_op jit(solution)/shard_map/convert_element_type | solution.py:125
  238.4 54.7 %all_to_all.16 = bf16[4,512,512]{2,1,0:T(8,128)(2,1)S(1)} all-to-all(bf16[4,512,512]{2,1,0:T(8,128)(2,1)S(1)} %multiply_convert_fusion), channel_id=1, replica_groups=mesh['seq'=8,'head'=4] {'head'}, dimensions={0} | all-to-all | bytes 4194304 | tf_op jit(solution)/shard_map/all_to_all | solution.py:127
  293.1 2.4 copy.97
  295.4 9.9 %convolution_convert_fusion = bf16[512,2048]{1,0:T(8,128)(2,1)} fusion(bf16[512,2048]{0,1:T(8,128)(2,1)} %bitcast.50, bf16[2048,2048]{1,0:T(8,128)(2,1)} %all-gather.4.cloned.1.call-done), kind=kOutput, calls=%fused_computation.37 | convolution fusion | flops 4296015872 | bytes 12582912 | tf_op jit(solution)/shard_map/dot_general | solution.py:128
  (46 shorter events, 11.5 us)
Async XLA Ops:
  6.5 200.7 %all-gather.6.cloned.1.call-start = ((), (), s32[]{:S(2)}) async-start(), calls=%async_computation.2 | async-start | bytes 2359296 | tf_op jit(solution)/shard_map/all_gather | solution.py:23
  14.2 8.8 %copy-start = (bf16[4,512,4,128]{3,2,1,0:T(4,128)(2,1)}, bf16[4,512,4,128]{3,2,1,0:T(4,128)(2,1)S(1)}, u32[]{:S(2)}) copy-start(bf16[4,512,4,128]{3,2,1,0:T(4,128)(2,1)S(1)} %reshape_reshape.11) | copy-start | bytes 6291460
  19.0 276.4 %all-gather.4.cloned.1.call-start = ((), (), s32[]{:S(2)}) async-start(), calls=%async_computation.1 | async-start | bytes 9437184 | tf_op jit(solution)/shard_map/all_gather | solution.py:130
  23.0 4.1 %slice-start = ((bf16[2048,512]{0,1:T(8,128)(2,1)}), bf16[1024,512]{0,1:T(8,128)(2,1)S(1)}, s32[]{:S(2)}) async-start(bf16[2048,512]{0,1:T(8,128)(2,1)} %copy.76), calls=%async_computation.3 | async-start | bytes 2097152 | tf_op jit(solution)/shard_map/slice | solution.py:81
  27.1 1.2 slice-start.1
  29.9 44.9 %collective-permute-start = (bf16[2,1024,4,128]{1,3,2,0:T(8,128)(2,1)}, bf16[2,1024,4,128]{1,3,2,0:T(8,128)(2,1)}, u32[]{:S(2)}, u32[]{:S(2)}) collective-permute-start(bf16[2,1024,4,128]{1,3,2,0:T(8,128)(2,1)} %pad_maximum_fusion.2), channel_id=1, source_target_pairs={{0,4},{4,8},{8,12},{12,16},{16,20},{20,24},{24,28},{1,5},{5,9},{9,... | collective-permute-start | bytes 6291464 | tf_op jit(solution)/shard_map/ppermute | solution.py:18
  51.5 12.9 %copy-start.6 = (f32[4,4,128,128]{3,2,1,0:T(8,128)S(1)}, f32[4,4,128,128]{3,2,1,0:T(8,128)}, u32[]{:S(2)}) copy-start(f32[4,4,128,128]{3,2,1,0:T(8,128)} %get-tuple-element.174) | copy-start | bytes 3145732
  74.8 2.2 copy-start.3
  74.8 2.9 copy-start.4
  207.2 1.1 copy-start.5
  208.4 2.2 copy-start.1
  208.4 3.5 %copy-start.2 = (f32[4,4,512,128]{2,3,1,0:T(8,128)S(1)}, f32[4,4,512,128]{2,3,1,0:T(8,128)}, u32[]{:S(2)}) copy-start(f32[4,4,512,128]{2,3,1,0:T(8,128)} %fusion.31) | copy-start | bytes 12582916
Sparse Core Ops, SparseCore 0:
  19.1 33.3 all-gather.5
  54.5 54.7 all-gather.3
where the time goes:
time: 316 us; the launch traced here: 312 us
  matrix products  135 us (43%)
  local copies, waits for them, and re-layouts  65.7 us (21%)
  blocking collectives  54.7 us (17%)
  other arithmetic  26.9 us (9%)
  between operations  13.5 us (4%)
  loops' own time  12.8 us (4%)
  starting transfers between devices  3.72 us (1%)
    all_to_all x1, blocking collectives, on_device(): lax.all_to_all(mixed_heads, 'head', split_axis=0, concat_axis=1, tiled=True)  54.7 us
    dot_general x4, matrix products, one_block(): jnp.einsum('hqk,khd->qhd', weights, value_block, preferred_element_type=j...  50.3 us
    dot_general x4, matrix products, one_block(): jnp.einsum('qhd,khd->hqk', query_block, key_block, preferred_element_type...  32.5 us
    mul x4, local copies, waits for them, and re-layouts, normalize(): branch * lax.rsqrt(jnp.mean(branch * branch, axis=-1, keepdims=True) + no...  18.7 us
    unnamed x17, local copies, waits for them, and re-layouts  16.7 us
    dot_general x1, matrix products, on_device(): jnp.einsum('bhqk,bkhd->bqhd', score_lower, blocked_values, preferred_elem...  12.9 us
    another operation x1, loops' own time, window_branch(): return lax.map(one_block, starts).reshape(tok_rows, heads_here, head_width)  12.8 us
    dot_general x1, matrix products, on_device(): jnp.einsum('bqhd,bkhd->bhqk', blocked_queries, blocked_keys, preferred_el...  11.3 us
  transfers between devices with their start and end apart: 3, of which 0 were waited for; matrix products, arithmetic and copies ran while one was open for 64% of the time, Pallas kernels for 0%

commit v1 on v0

v1 whole, which is shorter than its diff:
```python
import functools
import math

import jax
import jax.numpy as jnp
from jax import lax
from jax.experimental import pallas as pl
from jax.experimental.pallas import tpu as pltpu
from jax.sharding import PartitionSpec as P

HD = 128
W = 1024
NORM_EPS = 1e-06
F32 = jnp.float32
BF16 = jnp.bfloat16


def dot_nt(a, b):
    return lax.dot_general(a, b, (((1,), (1,)), ((), ())), preferred_element_type=F32)


def dot_tn(a, b):
    return lax.dot_general(a, b, (((0,), (0,)), ((), ())), preferred_element_type=F32)


def dot_nn(a, b):
    return jnp.dot(a, b, preferred_element_type=F32)


def normalize(branch):
    return branch * lax.rsqrt(jnp.mean(branch * branch, axis=-1, keepdims=True) + NORM_EPS)


def hi_lo(values):
    upper = values.astype(BF16)
    lower = (values - upper.astype(F32)).astype(BF16)
    return upper, lower


def totals_kernel(k_ref, v_ref, out_ref):
    for h in range(out_ref.shape[0]):
        cols = slice(h * HD, (h + 1) * HD)
        out_ref[h] = dot_tn(k_ref[:, cols], v_ref[:, cols])


def attend_block(q_ref, kbuf, vbuf, states, prior_ref, b, block, h, rows):
    cols = slice(h * HD, (h + 1) * HD)
    score_scale = math.log2(math.e) / math.sqrt(HD)
    q = q_ref[pl.ds(b, rows), cols]
    s = dot_nt(q, kbuf[pl.ds(b, W + rows), cols])
    row = lax.broadcasted_iota(jnp.int32, (rows, rows), 0)
    col = lax.broadcasted_iota(jnp.int32, (rows, rows), 1)
    raw = s[:, W:]
    first = jnp.where(col > row, s[:, :rows], -jnp.inf)
    last = jnp.where(col <= row, raw, -jnp.inf)
    s = jnp.concatenate([first, s[:, rows:W], last], axis=1)
    top = jnp.max(s, axis=-1, keepdims=True)
    p = jnp.exp2((s - top) * score_scale).astype(BF16)
    soft = dot_nn(p, vbuf[pl.ds(b, W + rows), cols])

    v_own = vbuf[pl.ds(b + W, rows), cols]
    upper, lower = hi_lo(jnp.where(col <= row, raw, 0.0))
    lin = dot_nn(upper, v_own) + dot_nn(lower, v_own)
    s_upper, s_lower = hi_lo(states[block, h] + prior_ref[h])
    lin += dot_nn(jnp.concatenate([q, q], axis=1), jnp.concatenate([s_upper, s_lower], axis=0))
    return (0.5 * (normalize(soft) + normalize(lin))).astype(BF16)


def attend_kernel(rows, q_ref, k_hbm, v_hbm, rim_hbm, prior_ref, out_ref, kbuf, vbuf, states, sems):
    tok_rows, width = q_ref.shape
    heads_here = width // HD
    blocks = tok_rows // rows
    copies = [
        pltpu.make_async_copy(k_hbm, kbuf.at[pl.ds(W, tok_rows)], sems.at[0]),
        pltpu.make_async_copy(v_hbm, vbuf.at[pl.ds(W, tok_rows)], sems.at[1]),
        pltpu.make_async_copy(rim_hbm.at[0], kbuf.at[pl.ds(0, W)], sems.at[2]),
        pltpu.make_async_copy(rim_hbm.at[1], vbuf.at[pl.ds(0, W)], sems.at[3]),
    ]
    for c in copies:
        c.start()
    for c in copies:
        c.wait()

    @pl.when(lax.axis_index("seq") == 0)
    def _():
        kbuf[0:W] = jnp.broadcast_to(kbuf[W : W + 1], (W, width))
        vbuf[0:W] = jnp.zeros((W, width), BF16)

    for h in range(heads_here):
        cols = slice(h * HD, (h + 1) * HD)
        total = jnp.zeros((HD, HD), F32)
        for block in range(blocks):
            states[block, h] = total
            span = slice(W + block * rows, W + (block + 1) * rows)
            if block < blocks - 1:
                total += dot_tn(kbuf[span, cols], vbuf[span, cols])

    def one_block(block, carry):
        b = pl.multiple_of(block * rows, rows)
        for h in range(heads_here):
            out_ref[pl.ds(b, rows), h * HD : (h + 1) * HD] = attend_block(
                q_ref, kbuf, vbuf, states, prior_ref, b, block, h, rows
            )
        return carry

    lax.fori_loop(0, blocks, one_block, 0)


def earlier_total(total, axis):
    count = lax.axis_size(axis)
    me = lax.axis_index(axis)
    prior = jnp.zeros_like(total)
    bit = 1
    while bit < count:
        other = lax.ppermute(total, axis, [(i, i ^ bit) for i in range(count)])
        prior = prior + jnp.where((me & bit) != 0, other, 0.0)
        total = total + other
        bit *= 2
    return prior


def on_device(queries, key_vectors, value_vectors, w_out):
    tok_rows, width = queries.shape
    heads_here = width // HD
    count = lax.axis_size("seq")
    rows = min(256, tok_rows // lax.axis_size("head"))
    vmem = pl.BlockSpec(memory_space=pltpu.VMEM)
    hbm = pl.BlockSpec(memory_space=pl.ANY)
    total = pl.pallas_call(
        totals_kernel,
        out_shape=jax.ShapeDtypeStruct((heads_here, HD, HD), F32),
        in_specs=[vmem, vmem],
        out_specs=vmem,
        compiler_params=pltpu.CompilerParams(vmem_limit_bytes=32 << 20),
    )(key_vectors, value_vectors)
    rim = jnp.stack([key_vectors[tok_rows - W :], value_vectors[tok_rows - W :]])
    rim = lax.ppermute(rim, "seq", [(i, i + 1) for i in range(count - 1)])
    prior = earlier_total(total, "seq")
    mixed = pl.pallas_call(
        functools.partial(attend_kernel, rows),
        out_shape=jax.ShapeDtypeStruct((tok_rows, width), BF16),
        in_specs=[vmem, hbm, hbm, hbm, vmem],
        out_specs=vmem,
        scratch_shapes=[
            pltpu.VMEM((W + tok_rows, width), BF16),
            pltpu.VMEM((W + tok_rows, width), BF16),
            pltpu.VMEM((tok_rows // rows, heads_here, HD, HD), F32),
            pltpu.SemaphoreType.DMA((4,)),
        ],
        compiler_params=pltpu.CompilerParams(vmem_limit_bytes=48 << 20),
        cost_estimate=pl.CostEstimate(
            flops=2 * 2 * tok_rows * 1400 * width, bytes_accessed=8 << 20, transcendentals=0
        ),
    )(queries, key_vectors, value_vectors, rim, prior)
    regrouped = lax.all_to_all(mixed, "head", split_axis=0, concat_axis=1, tiled=True)
    projected = jnp.dot(
        regrouped,
        lax.all_gather(w_out, "seq", axis=0, tiled=True),
        preferred_element_type=F32,
    )
    return projected.astype(BF16)


def solution(mesh):
    placed = (P("seq", "head"), P("seq", "head"), P("seq", "head"), P("seq", None))
    return jax.shard_map(
        on_device, mesh=mesh, in_specs=placed, out_specs=P(("seq", "head"), None), check_vma=False
    )
```

time: 316 us -> 162 us (0.51)
  the two profiles are of different devices: /device:TPU:0 before, /device:TPU:5 now
where the time goes in v1:
time: 162 us
  waiting for transfers between devices  61 us (38%)
  blocking collectives  36 us (22%)
  Pallas kernels  28.5 us (18%)
  between operations  13.5 us (8%)
  matrix products  9.1 us (6%)
  starting transfers between devices  7.72 us (5%)
  local copies, waits for them, and re-layouts  5.77 us (4%)
    ppermute x3, waiting for transfers between devices, earlier_total(): other = lax.ppermute(total, axis, [(i, i ^ bit) for i in range(count)])  60.3 us
    all_to_all x1, blocking collectives, on_device(): lax.all_to_all(mixed, 'head', split_axis=0, concat_axis=1, tiled=True)  36 us
    pallas_call x1, Pallas kernels, on_device(): pl.pallas_call(functools.partial(attend_kernel, rows), out_shape=jax.Shap...  27.7 us
    dot_general x1, matrix products, on_device(): jnp.dot(regrouped, lax.all_gather(w_out, 'seq', axis=0, tiled=True), pref...  9.1 us
    ppermute x1, starting transfers between devices, on_device(): rim = lax.ppermute(rim, 'seq', [(i, i + 1) for i in range(count - 1)])  3.94 us
    ppermute x3, starting transfers between devices, earlier_total(): other = lax.ppermute(total, axis, [(i, i ^ bit) for i in range(count)])  3.78 us
  transfers between devices with their start and end apart: 5, of which 3 were waited for; matrix products, arithmetic and copies ran while one was open for 3% of the time, Pallas kernels for 18%

profile of v1, /device:TPU:5, one launch (start us, length us, event | category | flops | bytes accessed | tf_op | source)
XLA Modules:
  0.0 161.8 jit_solution(5856167470453705625)
XLA Ops:
  6.5 0.0 all-gather.2.cloned.1.call-start
  6.5 0.7 all-gather.2.cloned.1.call-update
  7.3 1.7 %slice_bitcast_fusion = (bf16[1,1024,512]{2,1,0:T(8,128)(2,1)S(1)}, bf16[1,1024,512]{2,1,0:T(8,128)(2,1)S(1)}) fusion(bf16[2048,512]{1,0:T(8,128)(2,1)} %v_hbm.1, bf16[2048,512]{1,0:T(8,128)(2,1)} %k_hbm.1), kind=kLoop, calls=%fused_computation.2 | loop fusion | bytes 4194304 | tf_op jit(solution)/shard_map/stack | solution.py:136
  8.9 0.0 copy-start
  9.0 0.0 copy-start.1
  9.0 0.2 pad_maximum_fusion
  9.2 3.9 %collective-permute-start = (bf16[2,1024,512]{2,1,0:T(8,128)(2,1)S(1)}, bf16[2,1024,512]{2,1,0:T(8,128)(2,1)}, u32[]{:S(2)}, u32[]{:S(2)}) collective-permute-start(bf16[2,1024,512]{2,1,0:T(8,128)(2,1)S(1)} %pad_maximum_fusion), channel_id=1, source_target_pairs={{0,4},{4,8},{8,12},{12,16},{16,20},{20,24},{24,28},{1,5},{5,9},{9,... | collective-permute-start | bytes 6291464 | tf_op jit(solution)/shard_map/ppermute | solution.py:137
  13.1 0.0 copy-done
  13.1 0.0 copy-done.1
  13.1 0.8 shard_map.46
  13.9 0.1 collective-permute-start.1
  14.0 2.0 %collective-permute-done.1 = f32[4,128,128]{2,1,0:T(8,128)S(1)} collective-permute-done((f32[4,128,128]{2,1,0:T(8,128)S(1)}, f32[4,128,128]{2,1,0:T(8,128)S(1)}, u32[]{:S(2)}, u32[]{:S(2)}) %collective-permute-start.1) | collective-permute-done | bytes 262176 | tf_op jit(solution)/shard_map/ppermute | solution.py:115
  16.1 1.3 collective-permute-start.2
  17.3 48.5 %collective-permute-done.2 = f32[4,128,128]{2,1,0:T(8,128)S(1)} collective-permute-done((f32[4,128,128]{2,1,0:T(8,128)S(1)}, f32[4,128,128]{2,1,0:T(8,128)S(1)}, u32[]{:S(2)}, u32[]{:S(2)}) %collective-permute-start.2) | collective-permute-done | bytes 262176 | tf_op jit(solution)/shard_map/ppermute | solution.py:115
  65.9 2.4 %collective-permute-start.3 = (f32[4,128,128]{2,1,0:T(8,128)S(1)}, f32[4,128,128]{2,1,0:T(8,128)S(1)}, u32[]{:S(2)}, u32[]{:S(2)}) collective-permute-start(f32[4,128,128]{2,1,0:T(8,128)S(1)} %add.14), channel_id=1, source_target_pairs={{0,16},{4,20},{8,24},{12,28},{16,0},{20,4},{24,8},{28,12},{1,17},{... | collective-permute-start | bytes 786440 | tf_op jit(solution)/shard_map/ppermute | solution.py:115
  68.3 9.8 %collective-permute-done.3 = f32[4,128,128]{2,1,0:T(8,128)S(1)} collective-permute-done((f32[4,128,128]{2,1,0:T(8,128)S(1)}, f32[4,128,128]{2,1,0:T(8,128)S(1)}, u32[]{:S(2)}, u32[]{:S(2)}) %collective-permute-start.3) | collective-permute-done | bytes 262176 | tf_op jit(solution)/shard_map/ppermute | solution.py:115
  78.1 0.0 collective-permute-done.rim_hbm
  78.1 0.0 copy-start.2
  78.1 1.7 %copy-done.2 = bf16[2048,512]{1,0:T(8,128)(2,1)S(1)} copy-done((bf16[2048,512]{1,0:T(8,128)(2,1)S(1)}, bf16[2048,512]{1,0:T(8,128)(2,1)}, u32[]{:S(2)}) %copy-start.2) | copy-done | bytes 2097176
  79.8 27.7 %shard_map.47 = bf16[2048,512]{1,0:T(8,128)(2,1)S(1)} custom-call(bf16[2048,512]{1,0:T(8,128)(2,1)S(1)} %copy-done.2, bf16[2048,512]{1,0:T(8,128)(2,1)} %k_hbm.1, bf16[2048,512]{1,0:T(8,128)(2,1)} %v_hbm.1, bf16[2,1024,512]{2,1,0:T(8,128)(2,1)} %collective-permute-done.rim_hbm, f32[4,128,128]{2,1,0:T(8,128)S(1)} %select_add_fusion.prior_ref), custom_call_target="tpu_custom_call" | custom-call | flops 5872025600 | bytes 8388608 | tf_op jit(solution)/shard_map/pallas_call | solution.py:139
  107.5 2.4 %copy.5 = bf16[4,512,512]{1,2,0:T(8,128)(2,1)} copy(bf16[4,512,512]{2,1,0:T(8,128)(2,1)S(1)} %bitcast.10) | data formatting | bytes 4194304 | tf_op jit(solution)/shard_map/all_to_all | solution.py:155
  109.9 36.0 %all_to_all.19 = bf16[4,512,512]{1,2,0:T(8,128)(2,1)S(1)} all-to-all(bf16[4,512,512]{1,2,0:T(8,128)(2,1)} %copy.5), channel_id=1, replica_groups=mesh['seq'=8,'head'=4] {'head'}, dimensions={0} | all-to-all | bytes 4194304 | tf_op jit(solution)/shard_map/all_to_all | solution.py:155
  145.9 0.0 all-gather.2.cloned.1.call-done
  145.9 9.1 %convolution_convert_fusion = bf16[512,2048]{1,0:T(8,128)(2,1)} fusion(bf16[512,2048]{0,1:T(8,128)(2,1)S(1)} %bitcast.11, bf16[2048,2048]{1,0:T(8,128)(2,1)} %all-gather.2.cloned.1.call-done), kind=kOutput, calls=%fused_computation | convolution fusion | flops 4296015872 | bytes 12582912 | tf_op jit(solution)/shard_map/dot_general | solution.py:156
  (3 shorter events, 0.1 us)
Async XLA Ops:
  6.5 139.3 %all-gather.2.cloned.1.call-start = ((), (), s32[]{:S(2)}) async-start(), calls=%async_computation.1 | async-start | bytes 9437184 | tf_op jit(solution)/shard_map/all_gather | solution.py:158
  8.9 4.2 %copy-start = (bf16[2048,512]{1,0:T(8,128)(2,1)S(1)}, bf16[2048,512]{1,0:T(8,128)(2,1)}, u32[]{:S(2)}) copy-start(bf16[2048,512]{1,0:T(8,128)(2,1)} %k_hbm.1) | copy-start | bytes 6291460
  9.0 4.2 %copy-start.1 = (bf16[2048,512]{1,0:T(8,128)(2,1)S(1)}, bf16[2048,512]{1,0:T(8,128)(2,1)}, u32[]{:S(2)}) copy-start(bf16[2048,512]{1,0:T(8,128)(2,1)} %v_hbm.1) | copy-start | bytes 6291460
  9.2 68.9 %collective-permute-start = (bf16[2,1024,512]{2,1,0:T(8,128)(2,1)S(1)}, bf16[2,1024,512]{2,1,0:T(8,128)(2,1)}, u32[]{:S(2)}, u32[]{:S(2)}) collective-permute-start(bf16[2,1024,512]{2,1,0:T(8,128)(2,1)S(1)} %pad_maximum_fusion), channel_id=1, source_target_pairs={{0,4},{4,8},{8,12},{12,16},{16,20},{20,24},{24,28},{1,5},{5,9},{9,... | collective-permute-start | bytes 6291464 | tf_op jit(solution)/shard_map/ppermute | solution.py:137
  13.9 2.1 %collective-permute-start.1 = (f32[4,128,128]{2,1,0:T(8,128)S(1)}, f32[4,128,128]{2,1,0:T(8,128)S(1)}, u32[]{:S(2)}, u32[]{:S(2)}) collective-permute-start(f32[4,128,128]{2,1,0:T(8,128)S(1)} %shard_map.46), channel_id=1, source_target_pairs={{0,4},{4,0},{8,12},{12,8},{16,20},{20,16},{24,28},{28,24},{1,5},{5... | collective-permute-start | bytes 786440 | tf_op jit(solution)/shard_map/ppermute | solution.py:115
  16.1 49.8 %collective-permute-start.2 = (f32[4,128,128]{2,1,0:T(8,128)S(1)}, f32[4,128,128]{2,1,0:T(8,128)S(1)}, u32[]{:S(2)}, u32[]{:S(2)}) collective-permute-start(f32[4,128,128]{2,1,0:T(8,128)S(1)} %add.12), channel_id=1, source_target_pairs={{0,8},{4,12},{8,0},{12,4},{16,24},{20,28},{24,16},{28,20},{1,9},{5... | collective-permute-start | bytes 786440 | tf_op jit(solution)/shard_map/ppermute | solution.py:115
  65.9 12.2 %collective-permute-start.3 = (f32[4,128,128]{2,1,0:T(8,128)S(1)}, f32[4,128,128]{2,1,0:T(8,128)S(1)}, u32[]{:S(2)}, u32[]{:S(2)}) collective-permute-start(f32[4,128,128]{2,1,0:T(8,128)S(1)} %add.14), channel_id=1, source_target_pairs={{0,16},{4,20},{8,24},{12,28},{16,0},{20,4},{24,8},{28,12},{1,17},{... | collective-permute-start | bytes 786440 | tf_op jit(solution)/shard_map/ppermute | solution.py:115
  78.1 1.7 %copy-start.2 = (bf16[2048,512]{1,0:T(8,128)(2,1)S(1)}, bf16[2048,512]{1,0:T(8,128)(2,1)}, u32[]{:S(2)}) copy-start(bf16[2048,512]{1,0:T(8,128)(2,1)} %q_ref.1) | copy-start | bytes 6291460
Sparse Core Ops, SparseCore 0:
  9.2 70.9 all-gather.1

commit v2 on v1

v2 whole, which is shorter than its diff:
```python
import functools
import math

import jax
import jax.numpy as jnp
from jax import lax
from jax.experimental import pallas as pl
from jax.experimental.pallas import tpu as pltpu
from jax.sharding import PartitionSpec as P

HD = 128
W = 1024
NORM_EPS = 1e-06
F32 = jnp.float32
BF16 = jnp.bfloat16
MESH = pl.DeviceIdType.MESH


def dot_nt(a, b):
    return lax.dot_general(a, b, (((1,), (1,)), ((), ())), preferred_element_type=F32)


def dot_tn(a, b):
    return lax.dot_general(a, b, (((0,), (0,)), ((), ())), preferred_element_type=F32)


def dot_nn(a, b):
    return jnp.dot(a, b, preferred_element_type=F32)


def normalize(branch):
    return branch * lax.rsqrt(jnp.mean(branch * branch, axis=-1, keepdims=True) + NORM_EPS)


def hi_lo(values):
    upper = values.astype(BF16)
    lower = (values - upper.astype(F32)).astype(BF16)
    return upper, lower


def flip(index, bit):
    return index + bit - 2 * bit * lax.rem(lax.div(index, bit), 2)


def raw_block(q_ref, kbuf, vbuf, b, h, rows):
    cols = slice(h * HD, (h + 1) * HD)
    score_scale = math.log2(math.e) / math.sqrt(HD)
    q = q_ref[pl.ds(b, rows), cols]
    s = dot_nt(q, kbuf[pl.ds(b, W + rows), cols])
    row = lax.broadcasted_iota(jnp.int32, (rows, rows), 0)
    col = lax.broadcasted_iota(jnp.int32, (rows, rows), 1)
    raw = s[:, W:]
    first = jnp.where(col > row, s[:, :rows], -jnp.inf)
    last = jnp.where(col <= row, raw, -jnp.inf)
    s = jnp.concatenate([first, s[:, rows:W], last], axis=1)
    top = jnp.max(s, axis=-1, keepdims=True)
    p = jnp.exp2((s - top) * score_scale).astype(BF16)
    soft = dot_nn(p, vbuf[pl.ds(b, W + rows), cols])
    v_own = vbuf[pl.ds(b + W, rows), cols]
    upper, lower = hi_lo(jnp.where(col <= row, raw, 0.0))
    return normalize(soft), dot_nn(upper, v_own) + dot_nn(lower, v_own)


def mix_block(q_ref, states, prior, soft, lin, b, block, h, rows):
    q = q_ref[pl.ds(b, rows), h * HD : (h + 1) * HD]
    s_upper, s_lower = hi_lo(states[block, h] + prior[h])
    lin += dot_nn(jnp.concatenate([q, q], axis=1), jnp.concatenate([s_upper, s_lower], axis=0))
    return (0.5 * (soft + normalize(lin))).astype(BF16)


def layer_kernel(
    rows, shards, groups,
    q_ref, k_hbm, v_hbm, w_hbm, out_ref,
    kbuf, vbuf, states, prior, totals, arrived, soft_keep, lin_keep, mixed, regrouped, w_all,
    local_sem, state_send, state_recv, rim_send, rim_recv, w_send, w_recv, mix_send, mix_recv,
):
    tok_rows, width = q_ref.shape
    heads_here = width // HD
    blocks = tok_rows // rows
    rim_blocks = W // rows
    own_rows = tok_rows // groups
    subs = own_rows // rows
    w_rows = w_hbm.shape[0]
    rounds = shards.bit_length() - 1
    me = lax.axis_index("seq")
    group = lax.axis_index("head")

    local = [
        pltpu.make_async_copy(k_hbm, kbuf.at[pl.ds(W, tok_rows)], local_sem.at[0]),
        pltpu.make_async_copy(v_hbm, vbuf.at[pl.ds(W, tok_rows)], local_sem.at[1]),
        pltpu.make_async_copy(w_hbm, w_all.at[pl.ds(me * w_rows, w_rows)], local_sem.at[2]),
    ]
    for c in local:
        c.start()

    barrier = pltpu.get_barrier_semaphore()
    for step in range(1, groups):
        peer = lax.rem(group + step, groups)
        pl.semaphore_signal(barrier, inc=1, device_id={"head": peer}, device_id_type=MESH)
    for r in range(rounds):
        pl.semaphore_signal(barrier, inc=1, device_id={"seq": flip(me, 1 << r)}, device_id_type=MESH)
    for step in (1, shards - 1):
        pl.semaphore_signal(
            barrier, inc=1, device_id={"seq": lax.rem(me + step, shards)}, device_id_type=MESH
        )
    pl.semaphore_wait(barrier, groups - 1 + rounds + 2)

    def rim_copies(n):
        out = []
        for which, (hbm, buf) in enumerate(((k_hbm, kbuf), (v_hbm, vbuf))):
            out.append(
                pltpu.make_async_remote_copy(
                    src_ref=hbm.at[pl.ds(tok_rows - W + n * rows, rows)],
                    dst_ref=buf.at[pl.ds(n * rows, rows)],
                    send_sem=rim_send.at[which, n],
                    recv_sem=rim_recv.at[which, n],
                    device_id={"seq": lax.rem(me + 1, shards)},
                    device_id_type=MESH,
                )
            )
        return out

    @pl.when(me < shards - 1)
    def _():
        for n in reversed(range(rim_blocks)):
            for c in rim_copies(n):
                c.start()

    for c in local:
        c.wait()

    @pl.when(me == 0)
    def _():
        kbuf[0:W] = jnp.broadcast_to(kbuf[W : W + 1], (W, width))
        vbuf[0:W] = jnp.zeros((W, width), BF16)

    for h in range(heads_here):
        cols = slice(h * HD, (h + 1) * HD)
        total = jnp.zeros((HD, HD), F32)
        for block in range(blocks):
            states[block, h] = total
            span = slice(W + block * rows, W + (block + 1) * rows)
            total += dot_tn(kbuf[span, cols], vbuf[span, cols])
        totals[0, h] = total
    prior[...] = jnp.zeros_like(prior)

    def state_copy(r, bit):
        return pltpu.make_async_remote_copy(
            src_ref=totals.at[r],
            dst_ref=arrived.at[r],
            send_sem=state_send.at[r],
            recv_sem=state_recv.at[r],
            device_id={"seq": flip(me, bit)},
            device_id_type=MESH,
        )

    state_copy(0, 1).start()

    def block_at(i):
        plain = jnp.where(i < blocks - rim_blocks, rim_blocks + i, blocks - 1 - i)
        if blocks != 2 * rim_blocks:
            return plain
        half = lax.div(i, 2)
        spread = jnp.where(lax.rem(i, 2) == 0, rim_blocks + half, rim_blocks - 1 - half)
        return jnp.where(2 * group >= groups, spread, plain)

    def await_rim(block):
        @pl.when((block < rim_blocks) & (me > 0))
        def _():
            for c in rim_copies(lax.rem(block, rim_blocks)):
                c.wait_recv()

    def mix_copy(block, source, target):
        sub = lax.rem(block, subs)
        return pltpu.make_async_remote_copy(
            src_ref=mixed.at[pl.ds(block * rows, rows)],
            dst_ref=regrouped.at[pl.ds(sub * rows, rows), pl.ds(source * width, width)],
            send_sem=mix_send.at[block],
            recv_sem=mix_recv.at[source, sub],
            device_id={"head": target},
            device_id_type=MESH,
        )

    def hand_on(block):
        target = lax.div(block, subs)

        @pl.when(target != group)
        def _():
            mix_copy(block, group, target).start()

        @pl.when(target == group)
        def _():
            c = pltpu.make_async_copy(
                mixed.at[pl.ds(block * rows, rows)],
                regrouped.at[pl.ds(lax.rem(block, subs) * rows, rows), pl.ds(group * width, width)],
                local_sem.at[0],
            )
            c.start()
            c.wait()

    def early(i, bit):
        block = block_at(i)
        b = pl.multiple_of(block * rows, rows)
        await_rim(block)
        for h in range(heads_here):
            soft_keep[i, h], lin_keep[i, h] = raw_block(q_ref, kbuf, vbuf, b, h, rows)
        state_copy(i, bit).wait()
        later = lax.rem(lax.div(me, bit), 2).astype(F32)
        prior[...] += arrived[i] * later
        totals[i + 1] = totals[i] + arrived[i]

        @pl.when(i + 1 < rounds)
        def _():
            state_copy(i + 1, 2 * bit).start()

        return 2 * bit

    lax.fori_loop(0, rounds, early, jnp.int32(1))

    spread_bits = [1 << r for r in range(1, rounds)]
    have = [me]
    counter = [0]
    pending = []

    def w_copy(block, bit):
        n = counter[0]
        counter[0] += 1
        place = pl.ds(pl.multiple_of(block * w_rows, w_rows), w_rows)
        c = pltpu.make_async_remote_copy(
            src_ref=w_all.at[place],
            dst_ref=w_all.at[place],
            send_sem=w_send.at[n],
            recv_sem=w_recv.at[n],
            device_id={"seq": flip(me, bit)},
            device_id_type=MESH,
        )
        c.start()
        return c

    def w_round(r):
        if r > 0:
            for c in waiting:
                c.wait()
            waiting.clear()
        fresh = have[len(have) // 2 :] if r > 0 else have
        if r < len(spread_bits):
            bit = jnp.where(lax.rem(me, 2) == 0, spread_bits[r], spread_bits[len(spread_bits) - 1 - r])
            waiting.extend(w_copy(block, bit) for block in have)
        pending.extend(w_copy(block, 1) for block in fresh)
        if r < len(spread_bits):
            have.extend([flip(block, bit) for block in have])

    waiting = []
    w_round(0)

    def late_mix(i, carry):
        block = block_at(i)
        b = pl.multiple_of(block * rows, rows)
        for h in range(heads_here):
            mixed[pl.ds(b, rows), h * HD : (h + 1) * HD] = mix_block(
                q_ref, states, prior, soft_keep[i, h], lin_keep[i, h], b, block, h, rows
            )
        hand_on(block)
        return carry

    lax.fori_loop(0, rounds, late_mix, 0)

    def one_block(i, carry):
        block = block_at(i)
        b = pl.multiple_of(block * rows, rows)
        await_rim(block)
        for h in range(heads_here):
            soft, lin = raw_block(q_ref, kbuf, vbuf, b, h, rows)
            mixed[pl.ds(b, rows), h * HD : (h + 1) * HD] = mix_block(
                q_ref, states, prior, soft, lin, b, block, h, rows
            )
        hand_on(block)
        return carry

    middle = min(rounds + 2, blocks)
    lax.fori_loop(rounds, middle, one_block, 0)
    w_round(1)
    lax.fori_loop(middle, blocks, one_block, 0)
    for r in range(2, len(spread_bits) + 1):
        w_round(r)

    for c in pending:
        c.wait()
    for step in range(1, groups):
        source = lax.rem(group + step, groups)
        for sub in range(subs):
            mix_copy(sub, source, source).wait_recv()

    tile = 256

    def project(n, carry):
        cols = pl.ds(pl.multiple_of(n * tile, tile), tile)
        out_ref[:, cols] = dot_nn(regrouped[...], w_all[:, cols]).astype(BF16)
        return carry

    lax.fori_loop(0, out_ref.shape[1] // tile, project, 0)

    def sent(block, carry):
        target = lax.div(block, subs)

        @pl.when(target != group)
        def _():
            mix_copy(block, group, target).wait_send()

        return carry

    lax.fori_loop(0, blocks, sent, 0)

    @pl.when(me < shards - 1)
    def _():
        for n in range(rim_blocks):
            for c in rim_copies(n):
                c.wait_send()


def on_device(queries, key_vectors, value_vectors, w_out):
    tok_rows, width = queries.shape
    heads_here = width // HD
    shards = lax.axis_size("seq")
    groups = lax.axis_size("head")
    own_rows = tok_rows // groups
    rows = min(256, own_rows)
    w_rows, model = w_out.shape
    rounds = shards.bit_length() - 1
    vmem = pl.BlockSpec(memory_space=pltpu.VMEM)
    hbm = pl.BlockSpec(memory_space=pl.ANY)
    dma = pltpu.SemaphoreType.DMA
    return pl.pallas_call(
        functools.partial(layer_kernel, rows, shards, groups),
        out_shape=jax.ShapeDtypeStruct((own_rows, model), BF16),
        in_specs=[vmem, hbm, hbm, hbm],
        out_specs=vmem,
        scratch_shapes=[
            pltpu.VMEM((W + tok_rows, width), BF16),
            pltpu.VMEM((W + tok_rows, width), BF16),
            pltpu.VMEM((tok_rows // rows, heads_here, HD, HD), F32),
            pltpu.VMEM((heads_here, HD, HD), F32),
            pltpu.VMEM((rounds + 1, heads_here, HD, HD), F32),
            pltpu.VMEM((rounds, heads_here, HD, HD), F32),
            pltpu.VMEM((rounds, heads_here, rows, HD), F32),
            pltpu.VMEM((rounds, heads_here, rows, HD), F32),
            pltpu.VMEM((tok_rows, width), BF16),
            pltpu.VMEM((own_rows, groups * width), BF16),
            pltpu.VMEM((shards * w_rows, model), BF16),
            dma((3,)),
            dma((rounds,)),
            dma((rounds,)),
            dma((2, W // rows)),
            dma((2, W // rows)),
            dma((shards - 1,)),
            dma((shards - 1,)),
            dma((tok_rows // rows,)),
            dma((groups, own_rows // rows)),
        ],
        compiler_params=pltpu.CompilerParams(
            collective_id=0, has_side_effects=True, vmem_limit_bytes=56 << 20
        ),
        cost_estimate=pl.CostEstimate(
            flops=2 * tok_rows * 2800 * width + 2 * own_rows * model * model,
            bytes_accessed=16 << 20,
            transcendentals=0,
        ),
    )(queries, key_vectors, value_vectors, w_out)


def solution(mesh):
    placed = (P("seq", "head"), P("seq", "head"), P("seq", "head"), P("seq", None))
    return jax.shard_map(
        on_device, mesh=mesh, in_specs=placed, out_specs=P(("seq", "head"), None), check_vma=False
    )
```

time: 162 us -> 115 us (0.71)
  the two profiles are of different devices: /device:TPU:5 before, /device:TPU:0 now
where the time goes in v2:
time: 115 us
  Pallas kernels  112 us (97%)
  local copies, waits for them, and re-layouts  3.16 us (3%)
    pallas_call x1, Pallas kernels, on_device(): pl.pallas_call(functools.partial(layer_kernel, rows, shards, groups), out...  112 us
    unnamed x1, local copies, waits for them, and re-layouts  3.16 us

profile of v2, /device:TPU:0, one launch (start us, length us, event | category | flops | bytes accessed | tf_op | source)
XLA Modules:
  0.0 114.9 jit_solution(18192045371049007851)
XLA Ops:
  0.0 111.7 %shard_map.46 = bf16[512,2048]{1,0:T(8,128)(2,1)} custom-call(bf16[2048,512]{1,0:T(8,128)(2,1)} %q_ref.1, bf16[2048,512]{1,0:T(8,128)(2,1)} %k_hbm.1, bf16[2048,512]{1,0:T(8,128)(2,1)} %v_hbm.1, bf16[256,2048]{1,0:T(8,128)(2,1)} %w_hbm.1), custom_call_target="tpu_custom_call" | custom-call | flops 10166992896 | bytes 16777216 | tf_op jit(solution)/shard_map/pallas_call | solution.py:333
  111.7 3.2 %copy.6 = bf16[512,2048]{1,0:T(8,128)(2,1)} copy(bf16[512,2048]{1,0:T(8,128)(2,1)} %shard_map.46) | data formatting | bytes 4194304

commit v3 on v2

--- a/solution.py
+++ b/solution.py
@@ -71,7 +71,7 @@
 def layer_kernel(
     rows, shards, groups,
     q_ref, k_hbm, v_hbm, w_hbm, out_ref,
-    kbuf, vbuf, states, prior, totals, arrived, soft_keep, lin_keep, mixed, regrouped, w_all,
+    kbuf, vbuf, states, prior, totals, arrived, soft_keep, lin_keep, mixed, regrouped, w_all, sums,
     local_sem, state_send, state_recv, rim_send, rim_recv, w_send, w_recv, mix_send, mix_recv,
 ):
     tok_rows, width = q_ref.shape
@@ -120,103 +120,7 @@
             )
         return out
 
-    @pl.when(me < shards - 1)
-    def _():
-        for n in reversed(range(rim_blocks)):
-            for c in rim_copies(n):
-                c.start()
-
-    for c in local:
-        c.wait()
-
-    @pl.when(me == 0)
-    def _():
-        kbuf[0:W] = jnp.broadcast_to(kbuf[W : W + 1], (W, width))
-        vbuf[0:W] = jnp.zeros((W, width), BF16)
-
-    for h in range(heads_here):
-        cols = slice(h * HD, (h + 1) * HD)
-        total = jnp.zeros((HD, HD), F32)
-        for block in range(blocks):
-            states[block, h] = total
-            span = slice(W + block * rows, W + (block + 1) * rows)
-            total += dot_tn(kbuf[span, cols], vbuf[span, cols])
-        totals[0, h] = total
-    prior[...] = jnp.zeros_like(prior)
-
-    def state_copy(r, bit):
-        return pltpu.make_async_remote_copy(
-            src_ref=totals.at[r],
-            dst_ref=arrived.at[r],
-            send_sem=state_send.at[r],
-            recv_sem=state_recv.at[r],
-            device_id={"seq": flip(me, bit)},
-            device_id_type=MESH,
-        )
-
-    state_copy(0, 1).start()
-
-    def block_at(i):
-        plain = jnp.where(i < blocks - rim_blocks, rim_blocks + i, blocks - 1 - i)
-        if blocks != 2 * rim_blocks:
-            return plain
-        half = lax.div(i, 2)
-        spread = jnp.where(lax.rem(i, 2) == 0, rim_blocks + half, rim_blocks - 1 - half)
-        return jnp.where(2 * group >= groups, spread, plain)
-
-    def await_rim(block):
-        @pl.when((block < rim_blocks) & (me > 0))
-        def _():
-            for c in rim_copies(lax.rem(block, rim_blocks)):
-                c.wait_recv()
-
-    def mix_copy(block, source, target):
-        sub = lax.rem(block, subs)
-        return pltpu.make_async_remote_copy(
-            src_ref=mixed.at[pl.ds(block * rows, rows)],
-            dst_ref=regrouped.at[pl.ds(sub * rows, rows), pl.ds(source * width, width)],
-            send_sem=mix_send.at[block],
-            recv_sem=mix_recv.at[source, sub],
-            device_id={"head": target},
-            device_id_type=MESH,
-        )
-
-    def hand_on(block):
-        target = lax.div(block, subs)
-
-        @pl.when(target != group)
-        def _():
-            mix_copy(block, group, target).start()
-
-        @pl.when(target == group)
-        def _():
-            c = pltpu.make_async_copy(
-                mixed.at[pl.ds(block * rows, rows)],
-                regrouped.at[pl.ds(lax.rem(block, subs) * rows, rows), pl.ds(group * width, width)],
-                local_sem.at[0],
-            )
-            c.start()
-            c.wait()
-
-    def early(i, bit):
-        block = block_at(i)
-        b = pl.multiple_of(block * rows, rows)
-        await_rim(block)
-        for h in range(heads_here):
-            soft_keep[i, h], lin_keep[i, h] = raw_block(q_ref, kbuf, vbuf, b, h, rows)
-        state_copy(i, bit).wait()
-        later = lax.rem(lax.div(me, bit), 2).astype(F32)
-        prior[...] += arrived[i] * later
-        totals[i + 1] = totals[i] + arrived[i]
-
-        @pl.when(i + 1 < rounds)
-        def _():
-            state_copy(i + 1, 2 * bit).start()
-
-        return 2 * bit
-
-    lax.fori_loop(0, rounds, early, jnp.int32(1))
-
+    local[2].wait()
     spread_bits = [1 << r for r in range(1, rounds)]
     have = [me]
     counter = [0]
@@ -252,6 +156,111 @@
 
     waiting = []
     w_round(0)
+    for c in local[:2]:
+        c.wait()
+
+    @pl.when(me == 0)
+    def _():
+        kbuf[0:W] = jnp.broadcast_to(kbuf[W : W + 1], (W, width))
+        vbuf[0:W] = jnp.zeros((W, width), BF16)
+
+    for h in range(heads_here):
+        cols = slice(h * HD, (h + 1) * HD)
+        total = jnp.zeros((HD, HD), F32)
+        for block in range(blocks):
+            states[block, h] = total
+            span = slice(W + block * rows, W + (block + 1) * rows)
+            total += dot_tn(kbuf[span, cols], vbuf[span, cols])
+        totals[0, h] = total
+    prior[...] = jnp.zeros_like(prior)
+
+    def state_copy(r, bit):
+        return pltpu.make_async_remote_copy(
+            src_ref=totals.at[r],
+            dst_ref=arrived.at[r],
+            send_sem=state_send.at[r],
+            recv_sem=state_recv.at[r],
+            device_id={"seq": flip(me, bit)},
+            device_id_type=MESH,
+        )
+
+    state_copy(0, 1).start()
+
+    inner = list(range(rim_blocks, blocks))
+    outer = list(reversed(range(rim_blocks)))
+    plain = inner + outer
+    spread, inner = inner[:rounds], inner[rounds:]
+    while inner or outer:
+        spread += outer[:2] + inner[:1]
+        inner, outer = inner[1:], outer[2:]
+
+    def block_at(i):
+        block = 0
+        for j in range(blocks):
+            chosen = jnp.where(2 * group >= groups, spread[j], plain[j])
+            block = block + jnp.where(i == j, chosen, 0)
+        return block
+
+    def await_rim(block):
+        @pl.when((block < rim_blocks) & (me > 0))
+        def _():
+            for c in rim_copies(lax.rem(block, rim_blocks)):
+                c.wait_recv()
+
+    def mix_copy(block, source, target):
+        sub = lax.rem(block, subs)
+        return pltpu.make_async_remote_copy(
+            src_ref=mixed.at[pl.ds(block * rows, rows)],
+            dst_ref=regrouped.at[pl.ds(sub * rows, rows), pl.ds(source * width, width)],
+            send_sem=mix_send.at[block],
+            recv_sem=mix_recv.at[source, sub],
+            device_id={"head": target},
+            device_id_type=MESH,
+        )
+
+    def hand_on(block):
+        target = lax.div(block, subs)
+
+        @pl.when(target != group)
+        def _():
+            mix_copy(block, group, target).start()
+
+        @pl.when(target == group)
+        def _():
+            c = pltpu.make_async_copy(
+                mixed.at[pl.ds(block * rows, rows)],
+                regrouped.at[pl.ds(lax.rem(block, subs) * rows, rows), pl.ds(group * width, width)],
+                local_sem.at[0],
+            )
+            c.start()
+            c.wait()
+
+    def early(i, bit):
+        block = block_at(i)
+        b = pl.multiple_of(block * rows, rows)
+        await_rim(block)
+        for h in range(heads_here):
+            soft_keep[i, h], lin_keep[i, h] = raw_block(q_ref, kbuf, vbuf, b, h, rows)
+        state_copy(i, bit).wait()
+        later = lax.rem(lax.div(me, bit), 2).astype(F32)
+        prior[...] += arrived[i] * later
+        totals[i + 1] = totals[i] + arrived[i]
+
+        @pl.when(i + 1 < rounds)
+        def _():
+            state_copy(i + 1, 2 * bit).start()
+
+        @pl.when((i == 0) & (me < shards - 1))
+        def _():
+            for n in reversed(range(rim_blocks)):
+                for c in rim_copies(n):
+                    c.start()
+
+        return 2 * bit
+
+    lax.fori_loop(0, rounds, early, jnp.int32(1))
+
+    w_round(1)
 
     def late_mix(i, carry):
         block = block_at(i)
@@ -277,28 +286,35 @@
         hand_on(block)
         return carry
 
-    middle = min(rounds + 2, blocks)
-    lax.fori_loop(rounds, middle, one_block, 0)
-    w_round(1)
-    lax.fori_loop(middle, blocks, one_block, 0)
+    lax.fori_loop(rounds, blocks, one_block, 0)
     for r in range(2, len(spread_bits) + 1):
         w_round(r)
 
     for c in pending:
         c.wait()
-    for step in range(1, groups):
-        source = lax.rem(group + step, groups)
-        for sub in range(subs):
-            mix_copy(sub, source, source).wait_recv()
-
     tile = 256
-
-    def project(n, carry):
-        cols = pl.ds(pl.multiple_of(n * tile, tile), tile)
-        out_ref[:, cols] = dot_nn(regrouped[...], w_all[:, cols]).astype(BF16)
-        return carry
-
-    lax.fori_loop(0, out_ref.shape[1] // tile, project, 0)
+    for m in range(groups):
+        source = group
+        for r in range(groups.bit_length() - 1):
+            if m >> r & 1:
+                source = flip(source, 1 << r)
+        if m > 0:
+            for sub in range(subs):
+                mix_copy(sub, source, source).wait_recv()
+        held = pl.ds(pl.multiple_of(source * width, width), width)
+
+        def project(n, carry):
+            cols = pl.ds(pl.multiple_of(n * tile, tile), tile)
+            part = dot_nn(regrouped[:, held], w_all[held, cols])
+            if m > 0:
+                part += sums[:, cols]
+            if m < groups - 1:
+                sums[:, cols] = part
+            else:
+                out_ref[:, cols] = part.astype(BF16)
+            return carry
+
+        lax.fori_loop(0, out_ref.shape[1] // tile, project, 0)
 
     def sent(block, carry):
         target = lax.div(block, subs)
@@ -347,6 +363,7 @@
             pltpu.VMEM((tok_rows, width), BF16),
             pltpu.VMEM((own_rows, groups * width), BF16),
             pltpu.VMEM((shards * w_rows, model), BF16),
+            pltpu.VMEM((own_rows, model), F32),
             dma((3,)),
             dma((rounds,)),
             dma((rounds,)),

time: 115 us -> 96.3 us (0.84)
  Pallas kernels: 112 us -> 93 us
    pallas_call x1, Pallas kernels: 112 us -> 93 us  [on_device(): pl.pallas_call(functools.partial(layer_kernel, rows, shards, groups), out...]
where the time goes in v3:
time: 96.3 us; the launch traced here: 96.1 us
  Pallas kernels  93 us (97%)
  local copies, waits for them, and re-layouts  3.16 us (3%)
    pallas_call x1, Pallas kernels, on_device(): pl.pallas_call(functools.partial(layer_kernel, rows, shards, groups), out...  93 us
    unnamed x1, local copies, waits for them, and re-layouts  3.16 us

profile of v3, /device:TPU:0, one launch (start us, length us, event | category | flops | bytes accessed | tf_op | source)
XLA Modules:
  0.0 96.1 jit_solution(10433563078152447995)
XLA Ops:
  0.0 93.0 %shard_map.46 = bf16[512,2048]{1,0:T(8,128)(2,1)} custom-call(bf16[2048,512]{1,0:T(8,128)(2,1)} %q_ref.1, bf16[2048,512]{1,0:T(8,128)(2,1)} %k_hbm.1, bf16[2048,512]{1,0:T(8,128)(2,1)} %v_hbm.1, bf16[256,2048]{1,0:T(8,128)(2,1)} %w_hbm.1), custom_call_target="tpu_custom_call" | custom-call | flops 10166992896 | bytes 16777216 | tf_op jit(solution)/shard_map/pallas_call | solution.py:349
  93.0 3.2 %copy.6 = bf16[512,2048]{1,0:T(8,128)(2,1)} copy(bf16[512,2048]{1,0:T(8,128)(2,1)} %shard_map.46) | data formatting | bytes 4194304
